TPU v7x, 512 devices: a whole 4x8x8 slice. The times are simulated.
512 devices in a mesh: seq: 16 (over z, core), chan: 32 (over x, y).
Axes of the slice: x: 4, y: 8, z: 8, core: 2. Of those that a mesh axis runs over, the one named last changes fastest.
Arguments:
- tokens: bfloat16 [4096, 4096], P('seq', 'chan'), may hold values from -6 to 6
- w_in: bfloat16 [4096, 3, 4096], P(None, None, 'chan'), may hold values from -0.09375 to 0.09375
- filters: bfloat16 [256, 4096], P('chan'), may hold values from -0.09375 to 0.09375
- skip: float32 [4096], P('chan'), may hold values from 0.25 to 1.5
- w_out: bfloat16 [4096, 4096], P(None, 'chan'), may hold values from -0.09375 to 0.09375
Outputs:
- mixed: bfloat16 [4096, 4096], P('seq', 'chan')
All inputs are finite; a program needn't handle non-finite values.
Results may differ from a plain program's by a relative error of at most 0.015.
Values may be sent and summed in bfloat16 or wider, within the bound.
No kernel may reach another device: no remote copies, remote signals or barrier semaphores. Data moves between devices by JAX's collectives and lax.ppermute only.
A program may use at most 64 MiB of HBM per device.

v0:
```python
import math
import jax
import jax.numpy as jnp
from jax import lax
from jax.sharding import PartitionSpec as P


def toeplitz(padded, lead, offset, rows, cols):
    span = rows + cols
    segment = lax.dynamic_slice_in_dim(padded, lead + offset - cols + 1, span, 1)
    rolled = jnp.concatenate([segment[:, cols - 1 :], segment[:, : cols - 1]], axis=1)
    flat = jnp.tile(rolled, (1, cols))[:, : cols * (span - 1)]
    return flat.reshape(padded.shape[0], cols, span - 1)[:, :, :rows]


def apply_groups(matrix, values):
    groups = matrix.shape[0]
    grouped = values.reshape(values.shape[0], groups, -1)
    result = jnp.einsum("jgc,gji->gci", grouped, matrix, preferred_element_type=jnp.float32)
    return result.reshape(values.shape[1], matrix.shape[2]).T


def shards(tokens, w_in, filters, skip, w_out):
    block_len = tokens.shape[0]
    chans = w_out.shape[1]
    w_flat = w_in.reshape(w_in.shape[0], 3 * chans)
    rows = w_flat
    qkv = jnp.dot(
        lax.all_gather(tokens, "chan", axis=1, tiled=True), rows, preferred_element_type=jnp.float32
    )
    qkv = qkv.astype(jnp.bfloat16).reshape(block_len, 3, chans)
    query = qkv[:, 0]
    source = (qkv[:, 1].astype(jnp.float32) * qkv[:, 2].astype(jnp.float32)).astype(jnp.bfloat16)
    seq_rank = lax.axis_index("seq")
    lead = 2 * block_len
    row_first = seq_rank * block_len
    padded = jnp.pad(filters, ((0, 0), (lead, 1)))
    piece = lax.all_gather(source, "seq", axis=0, tiled=True)
    width = math.gcd(piece.shape[0], block_len)

    def visit(turn, carry):
        col_first = turn * width
        sub_block = lax.dynamic_slice_in_dim(piece, turn * width, width, 0)

        def contribute(acc):
            matrix = toeplitz(padded, lead, row_first - col_first, block_len, width)
            return acc + apply_groups(matrix, sub_block)

        return lax.cond(col_first < row_first + block_len, contribute, lambda acc: acc, carry)

    conv = lax.fori_loop(
        0, piece.shape[0] // width, visit, jnp.zeros((block_len, chans), jnp.float32)
    )
    gated = (
        query.astype(jnp.float32) * (conv + skip[None, :] * source.astype(jnp.float32))
    ).astype(jnp.bfloat16)
    rows = w_out
    mixed = jnp.dot(
        lax.all_gather(gated, "chan", axis=1, tiled=True), rows, preferred_element_type=jnp.float32
    )
    return mixed.astype(jnp.bfloat16)


def solution(mesh):
    in_specs = (
        P("seq", "chan"),
        P(None, None, "chan"),
        P("chan", None),
        P("chan"),
        P(None, "chan"),
    )
    out_specs = P("seq", "chan")
    return jax.shard_map(shards, mesh=mesh, in_specs=in_specs, out_specs=out_specs, check_vma=False)
```

profile of v0, /device:TPU:16, one launch (start us, length us, event | category | flops | bytes accessed | tf_op | source)
XLA Modules:
  0.0 409.9 jit_solution(13379084503499515155)
XLA Ops:
  6.5 0.0 copy-start
  6.5 0.0 all-gather.5.cloned.1.call-start
  6.5 0.7 all-gather.5.cloned.1.call-update
  7.3 0.0 all-gather.9.cloned.1.call-start
  7.3 4.7 %copy.9 = bf16[4096,3,128]{0,2,1:T(8,128)(2,1)} copy(bf16[4096,3,128]{2,0,1:T(8,128)(2,1)} %param.10) | data formatting | bytes 6291456 | tf_op args[1]
  12.0 82.4 %all-gather.5.cloned.1.call-done = bf16[256,4096]{1,0:T(8,128)(2,1)} async-done(((bf16[256,128]{1,0:T(8,128)(2,1)}), bf16[256,4096]{1,0:T(8,128)(2,1)}) %all-gather.5.cloned.1.call-update) | async-done | bytes 2097168 | tf_op jit(solution)/shard_map/all_gather | solution.py:29
  94.4 0.0 copy-start.1
  94.4 3.8 convolution_convert_fusion
  98.2 0.1 copy.10
  98.4 0.6 multiply_convert_fusion
  99.0 0.0 all-gather.9.cloned.1.call-update
  99.0 0.0 all-gather.7.cloned.1.call-start
  99.1 0.0 copy-done.1
  99.1 41.1 %all-gather.9.cloned.1.call-done = bf16[4096,1,128]{0,2,1:T(8,128)(2,1)} async-done(((bf16[256,1,128]{0,2,1:T(8,128)(2,1)}), bf16[4096,1,128]{0,2,1:T(8,128)(2,1)}) %all-gather.9.cloned.1.call-update) | async-done | bytes 1048592 | tf_op jit(solution)/shard_map/all_gather | solution.py:38
  140.2 0.0 copy-start.2
  140.2 11.8 %while.17 = (s32[]{:T(128)}, f32[256,128]{0,1:T(8,128)S(1)}, s32[]{:T(128)}, bf16[4096,128]{0,1:T(8,128)(2,1)}, s32[]{:T(128)}, /*index=5*/bf16[8,4609]{1,0:T(8,128)(2,1)S(1)}, s32[]{:T(128)}, s32[]{:T(128)}) while((s32[]{:T(128)}, f32[256,128]{0,1:T(8,128)S(1)}, s32[]{:T(128)}, bf16[4096,128]{0,1:T(8,128)(2,1)}, s32[]{:T(128)}, ...), condition=%wide.region_3.4_spmd, body=%wide.region_0.3_spmd.sunk | while | flops 16826380 | bytes 16466195 | solution.py:51
  140.3 11.2 %conditional.2 = (f32[256,128]{0,1:T(8,128)S(1)}) conditional(s32[]{:T(128)} %convert_element_type.67, f32[256,128]{0,1:T(8,128)S(1)} %get-tuple-element.249, (s32[]{:T(128)}, bf16[4096,128]{0,1:T(8,128)(2,1)}, s32[]{:T(128)}, bf16[8,4609]{1,0:T(8,128)(2,1)S(1)}, f32[256,128]{0,1:T(8,128)S(1)}) %tuple.50), branch_computations={%region_1.1_spmd, %region_2.2_spmd} | conditional | flops 16826376 | bytes 16466044 | solution.py:49
  140.3 0.1 constant_dynamic-slice_fusion
  140.4 0.1 constant_dynamic-slice_fusion.1
  140.5 0.1 pad_maximum_fusion
  140.5 0.1 tile.4
  140.7 0.1 slice.32
  140.8 4.4 %reshape.37 = bf16[1046528]{0:T(1024)(128)(2,1)} reshape(bf16[8,130816]{1,0:T(8,128)(2,1)S(1)} %slice.32) | data formatting | bytes 4186112 | tf_op jit(solution)/shard_map/while/body/eval_jaxpr/cond
  145.3 5.0 %reshape.28 = bf16[8,256,511]{2,1,0:T(8,128)(2,1)S(1)} reshape(bf16[1046528]{0:T(1024)(128)(2,1)} %reshape.37) | data formatting | bytes 4186112 | tf_op jit(solution)/shard_map/while/body/eval_jaxpr/cond/branch_1_fun/reshape | solution.py:13
  150.3 0.8 constant_dynamic-slice_fusion.2
  151.1 0.2 fusion
  152.1 0.0 copy-done.2
  152.1 0.7 fusion.4
  152.8 0.0 all-gather.7.cloned.1.call-update
  152.8 247.6 %all-gather.7.cloned.1.call-done = bf16[256,4096]{0,1:T(8,128)(2,1)} async-done(((bf16[256,128]{0,1:T(8,128)(2,1)}), bf16[256,4096]{0,1:T(8,128)(2,1)}) %all-gather.7.cloned.1.call-update) | async-done | bytes 2097168 | tf_op jit(solution)/shard_map/all_gather | solution.py:59
  400.4 0.0 copy-done
  400.4 3.0 convolution_convert_fusion.1
  (18 shorter events, 0.2 us)
Async XLA Ops:
  6.5 393.9 %copy-start = (bf16[4096,128]{1,0:T(8,128)(2,1)S(1)}, bf16[4096,128]{1,0:T(8,128)(2,1)}, u32[]{:S(2)}) copy-start(bf16[4096,128]{1,0:T(8,128)(2,1)} %param.13) | copy-start | bytes 3145732
  6.5 87.8 %all-gather.5.cloned.1.call-start = ((), (), s32[]{:S(2)}) async-start(), calls=%async_computation | async-start | bytes 2162688 | tf_op jit(solution)/shard_map/all_gather | solution.py:29
  7.3 133.0 %all-gather.9.cloned.1.call-start = ((), (), s32[]{:S(2)}) async-start(), calls=%async_computation.2 | async-start | bytes 1114112 | tf_op jit(solution)/shard_map/all_gather | solution.py:38
  94.4 4.7 %copy-start.1 = (bf16[8,4096]{1,0:T(8,128)(2,1)S(1)}, bf16[8,4096]{1,0:T(8,128)(2,1)}, u32[]{:S(2)}) copy-start(bf16[8,4096]{1,0:T(8,128)(2,1)} %param.11) | copy-start | bytes 196612
  99.0 301.4 %all-gather.7.cloned.1.call-start = ((), (), s32[]{:S(2)}) async-start(), calls=%async_computation.1 | async-start | bytes 2162688 | tf_op jit(solution)/shard_map/all_gather | solution.py:59
  140.2 11.8 %copy-start.2 = (f32[128]{0:T(128)S(1)}, f32[128]{0:T(128)}, u32[]{:S(2)}) copy-start(f32[128]{0:T(128)} %param.12) | copy-start | bytes 1540
Sparse Core Ops, SparseCore 0:
  10.4 83.9 all-gather.4
  99.1 41.0 all-gather.8
  152.9 247.4 all-gather.6
where the time goes:
time: 411 us; the launch traced here: 410 us
  waiting for transfers between devices  372 us (91%)
  local copies, waits for them, and re-layouts  15.6 us (4%)
  between operations  13.2 us (3%)
  matrix products  7.03 us (2%)
    all_gather x1, waiting for transfers between devices, shards(): lax.all_gather(gated, 'chan', axis=1, tiled=True)  248 us
    all_gather x1, waiting for transfers between devices, shards(): lax.all_gather(tokens, 'chan', axis=1, tiled=True)  82.4 us
    all_gather x1, waiting for transfers between devices, shards(): piece = lax.all_gather(source, 'seq', axis=0, tiled=True)  41.1 us
  transfers between devices with their start and end apart: 3, of which 3 were waited for; matrix products, arithmetic and copies ran while one was open for 1% of the time, Pallas kernels for 0%

commit v1 on v0

--- a/solution.py
+++ b/solution.py
@@ -3,6 +3,11 @@
 import jax.numpy as jnp
 from jax import lax
 from jax.sharding import PartitionSpec as P
+from jax.lax import all_to_all, axis_size
+
+raise_indices_on = lambda shard_in: jnp.concatenate(
+    all_to_all(jnp.stack(axis_size("chan") * [shard_in], 0), "chan", 0, 0), 1
+)
 
 
 def toeplitz(padded, lead, offset, rows, cols):
@@ -55,9 +60,7 @@
         query.astype(jnp.float32) * (conv + skip[None, :] * source.astype(jnp.float32))
     ).astype(jnp.bfloat16)
     rows = w_out
-    mixed = jnp.dot(
-        lax.all_gather(gated, "chan", axis=1, tiled=True), rows, preferred_element_type=jnp.float32
-    )
+    mixed = jnp.dot(raise_indices_on(gated), rows, preferred_element_type=jnp.float32)
     return mixed.astype(jnp.bfloat16)
 
 

time: 411 us -> 373 us (0.908)
  the two profiles are of different devices: /device:TPU:16 before, /device:TPU:457 now
where the time goes in v1:
time: 373 us; the launch traced here: 372 us
  local copies, waits for them, and re-layouts  177 us (47%)
  waiting for transfers between devices  118 us (32%)
  blocking collectives  50.5 us (14%)
  between operations  13.5 us (4%)
  matrix products  9.1 us (2%)
    reshape x16, local copies, waits for them, and re-layouts, toeplitz(): return flat.reshape(padded.shape[0], cols, span - 1)[:, :, :rows]  80.1 us
    all_gather x1, waiting for transfers between devices, shards(): lax.all_gather(tokens, 'chan', axis=1, tiled=True)  74.1 us
    cond x16, local copies, waits for them, and re-layouts  71.3 us
    all_to_all x1, blocking collectives, all_to_all(jnp.stack(axis_size('chan') * [shard_in], 0), 'chan', 0, 0)  50.5 us
    all_gather x1, waiting for transfers between devices, shards(): piece = lax.all_gather(source, 'seq', axis=0, tiled=True)  43.2 us
    dynamic_slice x16, local copies, waits for them, and re-layouts, visit(): sub_block = lax.dynamic_slice_in_dim(piece, turn * width, width, 0)  13.6 us
  transfers between devices with their start and end apart: 2, of which 2 were waited for; matrix products, arithmetic and copies ran while one was open for 1% of the time, Pallas kernels for 0%

profile of v1, /device:TPU:457, one launch (start us, length us, event | category | flops | bytes accessed | tf_op | source)
XLA Modules:
  0.0 372.2 jit_solution(7843591933172562167)
XLA Ops:
  7.3 4.7 %copy.10 = bf16[4096,3,128]{0,2,1:T(8,128)(2,1)} copy(bf16[4096,3,128]{2,0,1:T(8,128)(2,1)} %param.10) | data formatting | bytes 6291456 | tf_op args[1]
  12.0 74.1 %all-gather.4.cloned.1.call-done = bf16[256,4096]{1,0:T(8,128)(2,1)} async-done(((bf16[256,128]{1,0:T(8,128)(2,1)}), bf16[256,4096]{1,0:T(8,128)(2,1)}) %all-gather.4.cloned.1.call-update) | async-done | bytes 2097168 | tf_op jit(solution)/shard_map/all_gather | solution.py:34
  90.8 43.2 %all-gather.6.cloned.1.call-done = bf16[4096,1,128]{0,2,1:T(8,128)(2,1)} async-done(((bf16[256,1,128]{0,2,1:T(8,128)(2,1)}), bf16[4096,1,128]{0,2,1:T(8,128)(2,1)}) %all-gather.6.cloned.1.call-update) | async-done | bytes 1048592 | tf_op jit(solution)/shard_map/all_gather | solution.py:43
  134.1 179.0 %while.17 = (s32[]{:T(128)}, f32[256,128]{0,1:T(8,128)S(1)}, s32[]{:T(128)}, bf16[4096,128]{0,1:T(8,128)(2,1)}, s32[]{:T(128)}, /*index=5*/bf16[8,4609]{1,0:T(8,128)(2,1)S(1)}, s32[]{:T(128)}, s32[]{:T(128)}) while((s32[]{:T(128)}, f32[256,128]{0,1:T(8,128)S(1)}, s32[]{:T(128)}, bf16[4096,128]{0,1:T(8,128)(2,1)}, s32[]{:T(128)}, ...), condition=%wide.region_3.4_spmd, body=%wide.region_0.3_spmd.sunk | while | flops 16826380 | bytes 16466195 | solution.py:56
  134.1 11.2 %conditional.2 = (f32[256,128]{0,1:T(8,128)S(1)}) conditional(s32[]{:T(128)} %convert_element_type.67, f32[256,128]{0,1:T(8,128)S(1)} %get-tuple-element.249, (s32[]{:T(128)}, bf16[4096,128]{0,1:T(8,128)(2,1)}, s32[]{:T(128)}, bf16[8,4609]{1,0:T(8,128)(2,1)S(1)}, f32[256,128]{0,1:T(8,128)S(1)}) %tuple.50), branch_computations={%region_1.1_spmd, %region_2.2_spmd} | conditional | flops 16826376 | bytes 16466044 | solution.py:54
  134.6 4.5 %reshape.47 = bf16[1046528]{0:T(1024)(128)(2,1)} reshape(bf16[8,130816]{1,0:T(8,128)(2,1)S(1)} %slice.32) | data formatting | bytes 4186112 | tf_op jit(solution)/shard_map/while/body/eval_jaxpr/cond
  139.1 5.0 %reshape.34 = bf16[8,256,511]{2,1,0:T(8,128)(2,1)S(1)} reshape(bf16[1046528]{0:T(1024)(128)(2,1)} %reshape.47) | data formatting | bytes 4186112 | tf_op jit(solution)/shard_map/while/body/eval_jaxpr/cond/branch_1_fun/reshape | solution.py:18
  145.3 11.2 %conditional.2 = (f32[256,128]{0,1:T(8,128)S(1)}) conditional(s32[]{:T(128)} %convert_element_type.67, f32[256,128]{0,1:T(8,128)S(1)} %get-tuple-element.249, (s32[]{:T(128)}, bf16[4096,128]{0,1:T(8,128)(2,1)}, s32[]{:T(128)}, bf16[8,4609]{1,0:T(8,128)(2,1)S(1)}, f32[256,128]{0,1:T(8,128)S(1)}) %tuple.50), branch_computations={%region_1.1_spmd, %region_2.2_spmd} | conditional | flops 16826376 | bytes 16466044 | solution.py:54
  145.8 4.5 %reshape.47 = bf16[1046528]{0:T(1024)(128)(2,1)} reshape(bf16[8,130816]{1,0:T(8,128)(2,1)S(1)} %slice.32) | data formatting | bytes 4186112 | tf_op jit(solution)/shard_map/while/body/eval_jaxpr/cond
  150.3 5.0 %reshape.34 = bf16[8,256,511]{2,1,0:T(8,128)(2,1)S(1)} reshape(bf16[1046528]{0:T(1024)(128)(2,1)} %reshape.47) | data formatting | bytes 4186112 | tf_op jit(solution)/shard_map/while/body/eval_jaxpr/cond/branch_1_fun/reshape | solution.py:18
  156.5 11.2 %conditional.2 = (f32[256,128]{0,1:T(8,128)S(1)}) conditional(s32[]{:T(128)} %convert_element_type.67, f32[256,128]{0,1:T(8,128)S(1)} %get-tuple-element.249, (s32[]{:T(128)}, bf16[4096,128]{0,1:T(8,128)(2,1)}, s32[]{:T(128)}, bf16[8,4609]{1,0:T(8,128)(2,1)S(1)}, f32[256,128]{0,1:T(8,128)S(1)}) %tuple.50), branch_computations={%region_1.1_spmd, %region_2.2_spmd} | conditional | flops 16826376 | bytes 16466044 | solution.py:54
  157.0 4.5 %reshape.47 = bf16[1046528]{0:T(1024)(128)(2,1)} reshape(bf16[8,130816]{1,0:T(8,128)(2,1)S(1)} %slice.32) | data formatting | bytes 4186112 | tf_op jit(solution)/shard_map/while/body/eval_jaxpr/cond
  161.5 5.0 %reshape.34 = bf16[8,256,511]{2,1,0:T(8,128)(2,1)S(1)} reshape(bf16[1046528]{0:T(1024)(128)(2,1)} %reshape.47) | data formatting | bytes 4186112 | tf_op jit(solution)/shard_map/while/body/eval_jaxpr/cond/branch_1_fun/reshape | solution.py:18
  167.6 11.2 %conditional.2 = (f32[256,128]{0,1:T(8,128)S(1)}) conditional(s32[]{:T(128)} %convert_element_type.67, f32[256,128]{0,1:T(8,128)S(1)} %get-tuple-element.249, (s32[]{:T(128)}, bf16[4096,128]{0,1:T(8,128)(2,1)}, s32[]{:T(128)}, bf16[8,4609]{1,0:T(8,128)(2,1)S(1)}, f32[256,128]{0,1:T(8,128)S(1)}) %tuple.50), branch_computations={%region_1.1_spmd, %region_2.2_spmd} | conditional | flops 16826376 | bytes 16466044 | solution.py:54
  168.2 4.5 %reshape.47 = bf16[1046528]{0:T(1024)(128)(2,1)} reshape(bf16[8,130816]{1,0:T(8,128)(2,1)S(1)} %slice.32) | data formatting | bytes 4186112 | tf_op jit(solution)/shard_map/while/body/eval_jaxpr/cond
  172.7 5.0 %reshape.34 = bf16[8,256,511]{2,1,0:T(8,128)(2,1)S(1)} reshape(bf16[1046528]{0:T(1024)(128)(2,1)} %reshape.47) | data formatting | bytes 4186112 | tf_op jit(solution)/shard_map/while/body/eval_jaxpr/cond/branch_1_fun/reshape | solution.py:18
  178.8 11.2 %conditional.2 = (f32[256,128]{0,1:T(8,128)S(1)}) conditional(s32[]{:T(128)} %convert_element_type.67, f32[256,128]{0,1:T(8,128)S(1)} %get-tuple-element.249, (s32[]{:T(128)}, bf16[4096,128]{0,1:T(8,128)(2,1)}, s32[]{:T(128)}, bf16[8,4609]{1,0:T(8,128)(2,1)S(1)}, f32[256,128]{0,1:T(8,128)S(1)}) %tuple.50), branch_computations={%region_1.1_spmd, %region_2.2_spmd} | conditional | flops 16826376 | bytes 16466044 | solution.py:54
  179.4 4.5 %reshape.47 = bf16[1046528]{0:T(1024)(128)(2,1)} reshape(bf16[8,130816]{1,0:T(8,128)(2,1)S(1)} %slice.32) | data formatting | bytes 4186112 | tf_op jit(solution)/shard_map/while/body/eval_jaxpr/cond
  183.8 5.0 %reshape.34 = bf16[8,256,511]{2,1,0:T(8,128)(2,1)S(1)} reshape(bf16[1046528]{0:T(1024)(128)(2,1)} %reshape.47) | data formatting | bytes 4186112 | tf_op jit(solution)/shard_map/while/body/eval_jaxpr/cond/branch_1_fun/reshape | solution.py:18
  190.0 11.2 %conditional.2 = (f32[256,128]{0,1:T(8,128)S(1)}) conditional(s32[]{:T(128)} %convert_element_type.67, f32[256,128]{0,1:T(8,128)S(1)} %get-tuple-element.249, (s32[]{:T(128)}, bf16[4096,128]{0,1:T(8,128)(2,1)}, s32[]{:T(128)}, bf16[8,4609]{1,0:T(8,128)(2,1)S(1)}, f32[256,128]{0,1:T(8,128)S(1)}) %tuple.50), branch_computations={%region_1.1_spmd, %region_2.2_spmd} | conditional | flops 16826376 | bytes 16466044 | solution.py:54
  190.6 4.5 %reshape.47 = bf16[1046528]{0:T(1024)(128)(2,1)} reshape(bf16[8,130816]{1,0:T(8,128)(2,1)S(1)} %slice.32) | data formatting | bytes 4186112 | tf_op jit(solution)/shard_map/while/body/eval_jaxpr/cond
  195.0 5.0 %reshape.34 = bf16[8,256,511]{2,1,0:T(8,128)(2,1)S(1)} reshape(bf16[1046528]{0:T(1024)(128)(2,1)} %reshape.47) | data formatting | bytes 4186112 | tf_op jit(solution)/shard_map/while/body/eval_jaxpr/cond/branch_1_fun/reshape | solution.py:18
  201.2 11.2 %conditional.2 = (f32[256,128]{0,1:T(8,128)S(1)}) conditional(s32[]{:T(128)} %convert_element_type.67, f32[256,128]{0,1:T(8,128)S(1)} %get-tuple-element.249, (s32[]{:T(128)}, bf16[4096,128]{0,1:T(8,128)(2,1)}, s32[]{:T(128)}, bf16[8,4609]{1,0:T(8,128)(2,1)S(1)}, f32[256,128]{0,1:T(8,128)S(1)}) %tuple.50), branch_computations={%region_1.1_spmd, %region_2.2_spmd} | conditional | flops 16826376 | bytes 16466044 | solution.py:54
  201.8 4.5 %reshape.47 = bf16[1046528]{0:T(1024)(128)(2,1)} reshape(bf16[8,130816]{1,0:T(8,128)(2,1)S(1)} %slice.32) | data formatting | bytes 4186112 | tf_op jit(solution)/shard_map/while/body/eval_jaxpr/cond
  206.2 5.0 %reshape.34 = bf16[8,256,511]{2,1,0:T(8,128)(2,1)S(1)} reshape(bf16[1046528]{0:T(1024)(128)(2,1)} %reshape.47) | data formatting | bytes 4186112 | tf_op jit(solution)/shard_map/while/body/eval_jaxpr/cond/branch_1_fun/reshape | solution.py:18
  212.4 11.2 %conditional.2 = (f32[256,128]{0,1:T(8,128)S(1)}) conditional(s32[]{:T(128)} %convert_element_type.67, f32[256,128]{0,1:T(8,128)S(1)} %get-tuple-element.249, (s32[]{:T(128)}, bf16[4096,128]{0,1:T(8,128)(2,1)}, s32[]{:T(128)}, bf16[8,4609]{1,0:T(8,128)(2,1)S(1)}, f32[256,128]{0,1:T(8,128)S(1)}) %tuple.50), branch_computations={%region_1.1_spmd, %region_2.2_spmd} | conditional | flops 16826376 | bytes 16466044 | solution.py:54
  213.0 4.5 %reshape.47 = bf16[1046528]{0:T(1024)(128)(2,1)} reshape(bf16[8,130816]{1,0:T(8,128)(2,1)S(1)} %slice.32) | data formatting | bytes 4186112 | tf_op jit(solution)/shard_map/while/body/eval_jaxpr/cond
  217.4 5.0 %reshape.34 = bf16[8,256,511]{2,1,0:T(8,128)(2,1)S(1)} reshape(bf16[1046528]{0:T(1024)(128)(2,1)} %reshape.47) | data formatting | bytes 4186112 | tf_op jit(solution)/shard_map/while/body/eval_jaxpr/cond/branch_1_fun/reshape | solution.py:18
  223.6 11.2 %conditional.2 = (f32[256,128]{0,1:T(8,128)S(1)}) conditional(s32[]{:T(128)} %convert_element_type.67, f32[256,128]{0,1:T(8,128)S(1)} %get-tuple-element.249, (s32[]{:T(128)}, bf16[4096,128]{0,1:T(8,128)(2,1)}, s32[]{:T(128)}, bf16[8,4609]{1,0:T(8,128)(2,1)S(1)}, f32[256,128]{0,1:T(8,128)S(1)}) %tuple.50), branch_computations={%region_1.1_spmd, %region_2.2_spmd} | conditional | flops 16826376 | bytes 16466044 | solution.py:54
  224.2 4.5 %reshape.47 = bf16[1046528]{0:T(1024)(128)(2,1)} reshape(bf16[8,130816]{1,0:T(8,128)(2,1)S(1)} %slice.32) | data formatting | bytes 4186112 | tf_op jit(solution)/shard_map/while/body/eval_jaxpr/cond
  228.6 5.0 %reshape.34 = bf16[8,256,511]{2,1,0:T(8,128)(2,1)S(1)} reshape(bf16[1046528]{0:T(1024)(128)(2,1)} %reshape.47) | data formatting | bytes 4186112 | tf_op jit(solution)/shard_map/while/body/eval_jaxpr/cond/branch_1_fun/reshape | solution.py:18
  234.8 11.2 %conditional.2 = (f32[256,128]{0,1:T(8,128)S(1)}) conditional(s32[]{:T(128)} %convert_element_type.67, f32[256,128]{0,1:T(8,128)S(1)} %get-tuple-element.249, (s32[]{:T(128)}, bf16[4096,128]{0,1:T(8,128)(2,1)}, s32[]{:T(128)}, bf16[8,4609]{1,0:T(8,128)(2,1)S(1)}, f32[256,128]{0,1:T(8,128)S(1)}) %tuple.50), branch_computations={%region_1.1_spmd, %region_2.2_spmd} | conditional | flops 16826376 | bytes 16466044 | solution.py:54
  235.3 4.5 %reshape.47 = bf16[1046528]{0:T(1024)(128)(2,1)} reshape(bf16[8,130816]{1,0:T(8,128)(2,1)S(1)} %slice.32) | data formatting | bytes 4186112 | tf_op jit(solution)/shard_map/while/body/eval_jaxpr/cond
  239.8 5.0 %reshape.34 = bf16[8,256,511]{2,1,0:T(8,128)(2,1)S(1)} reshape(bf16[1046528]{0:T(1024)(128)(2,1)} %reshape.47) | data formatting | bytes 4186112 | tf_op jit(solution)/shard_map/while/body/eval_jaxpr/cond/branch_1_fun/reshape | solution.py:18
  246.0 11.2 %conditional.2 = (f32[256,128]{0,1:T(8,128)S(1)}) conditional(s32[]{:T(128)} %convert_element_type.67, f32[256,128]{0,1:T(8,128)S(1)} %get-tuple-element.249, (s32[]{:T(128)}, bf16[4096,128]{0,1:T(8,128)(2,1)}, s32[]{:T(128)}, bf16[8,4609]{1,0:T(8,128)(2,1)S(1)}, f32[256,128]{0,1:T(8,128)S(1)}) %tuple.50), branch_computations={%region_1.1_spmd, %region_2.2_spmd} | conditional | flops 16826376 | bytes 16466044 | solution.py:54
  246.5 4.5 %reshape.47 = bf16[1046528]{0:T(1024)(128)(2,1)} reshape(bf16[8,130816]{1,0:T(8,128)(2,1)S(1)} %slice.32) | data formatting | bytes 4186112 | tf_op jit(solution)/shard_map/while/body/eval_jaxpr/cond
  251.0 5.0 %reshape.34 = bf16[8,256,511]{2,1,0:T(8,128)(2,1)S(1)} reshape(bf16[1046528]{0:T(1024)(128)(2,1)} %reshape.47) | data formatting | bytes 4186112 | tf_op jit(solution)/shard_map/while/body/eval_jaxpr/cond/branch_1_fun/reshape | solution.py:18
  257.2 11.2 %conditional.2 = (f32[256,128]{0,1:T(8,128)S(1)}) conditional(s32[]{:T(128)} %convert_element_type.67, f32[256,128]{0,1:T(8,128)S(1)} %get-tuple-element.249, (s32[]{:T(128)}, bf16[4096,128]{0,1:T(8,128)(2,1)}, s32[]{:T(128)}, bf16[8,4609]{1,0:T(8,128)(2,1)S(1)}, f32[256,128]{0,1:T(8,128)S(1)}) %tuple.50), branch_computations={%region_1.1_spmd, %region_2.2_spmd} | conditional | flops 16826376 | bytes 16466044 | solution.py:54
  262.2 5.0 %reshape.34 = bf16[8,256,511]{2,1,0:T(8,128)(2,1)S(1)} reshape(bf16[1046528]{0:T(1024)(128)(2,1)} %reshape.47) | data formatting | bytes 4186112 | tf_op jit(solution)/shard_map/while/body/eval_jaxpr/cond/branch_1_fun/reshape | solution.py:18
  268.4 11.2 %conditional.2 = (f32[256,128]{0,1:T(8,128)S(1)}) conditional(s32[]{:T(128)} %convert_element_type.67, f32[256,128]{0,1:T(8,128)S(1)} %get-tuple-element.249, (s32[]{:T(128)}, bf16[4096,128]{0,1:T(8,128)(2,1)}, s32[]{:T(128)}, bf16[8,4609]{1,0:T(8,128)(2,1)S(1)}, f32[256,128]{0,1:T(8,128)S(1)}) %tuple.50), branch_computations={%region_1.1_spmd, %region_2.2_spmd} | conditional | flops 16826376 | bytes 16466044 | solution.py:54
  273.4 5.0 %reshape.34 = bf16[8,256,511]{2,1,0:T(8,128)(2,1)S(1)} reshape(bf16[1046528]{0:T(1024)(128)(2,1)} %reshape.47) | data formatting | bytes 4186112 | tf_op jit(solution)/shard_map/while/body/eval_jaxpr/cond/branch_1_fun/reshape | solution.py:18
  279.5 11.2 %conditional.2 = (f32[256,128]{0,1:T(8,128)S(1)}) conditional(s32[]{:T(128)} %convert_element_type.67, f32[256,128]{0,1:T(8,128)S(1)} %get-tuple-element.249, (s32[]{:T(128)}, bf16[4096,128]{0,1:T(8,128)(2,1)}, s32[]{:T(128)}, bf16[8,4609]{1,0:T(8,128)(2,1)S(1)}, f32[256,128]{0,1:T(8,128)S(1)}) %tuple.50), branch_computations={%region_1.1_spmd, %region_2.2_spmd} | conditional | flops 16826376 | bytes 16466044 | solution.py:54
  284.6 5.0 %reshape.34 = bf16[8,256,511]{2,1,0:T(8,128)(2,1)S(1)} reshape(bf16[1046528]{0:T(1024)(128)(2,1)} %reshape.47) | data formatting | bytes 4186112 | tf_op jit(solution)/shard_map/while/body/eval_jaxpr/cond/branch_1_fun/reshape | solution.py:18
  290.7 11.2 %conditional.2 = (f32[256,128]{0,1:T(8,128)S(1)}) conditional(s32[]{:T(128)} %convert_element_type.67, f32[256,128]{0,1:T(8,128)S(1)} %get-tuple-element.249, (s32[]{:T(128)}, bf16[4096,128]{0,1:T(8,128)(2,1)}, s32[]{:T(128)}, bf16[8,4609]{1,0:T(8,128)(2,1)S(1)}, f32[256,128]{0,1:T(8,128)S(1)}) %tuple.50), branch_computations={%region_1.1_spmd, %region_2.2_spmd} | conditional | flops 16826376 | bytes 16466044 | solution.py:54
  295.7 5.0 %reshape.34 = bf16[8,256,511]{2,1,0:T(8,128)(2,1)S(1)} reshape(bf16[1046528]{0:T(1024)(128)(2,1)} %reshape.47) | data formatting | bytes 4186112 | tf_op jit(solution)/shard_map/while/body/eval_jaxpr/cond/branch_1_fun/reshape | solution.py:18
  301.9 11.2 %conditional.2 = (f32[256,128]{0,1:T(8,128)S(1)}) conditional(s32[]{:T(128)} %convert_element_type.67, f32[256,128]{0,1:T(8,128)S(1)} %get-tuple-element.249, (s32[]{:T(128)}, bf16[4096,128]{0,1:T(8,128)(2,1)}, s32[]{:T(128)}, bf16[8,4609]{1,0:T(8,128)(2,1)S(1)}, f32[256,128]{0,1:T(8,128)S(1)}) %tuple.50), branch_computations={%region_1.1_spmd, %region_2.2_spmd} | conditional | flops 16826376 | bytes 16466044 | solution.py:54
  306.9 5.0 %reshape.34 = bf16[8,256,511]{2,1,0:T(8,128)(2,1)S(1)} reshape(bf16[1046528]{0:T(1024)(128)(2,1)} %reshape.47) | data formatting | bytes 4186112 | tf_op jit(solution)/shard_map/while/body/eval_jaxpr/cond/branch_1_fun/reshape | solution.py:18
  313.4 50.5 %all_to_all.5 = bf16[32,256,128]{1,2,0:T(8,128)(2,1)S(1)} all-to-all(bf16[32,256,128]{1,2,0:T(8,128)(2,1)S(1)} %stack.2), channel_id=1, replica_groups=mesh['seq'=16,'chan'=32] {'chan'}, dimensions={0} | all-to-all | bytes 4194304 | tf_op jit(solution)/shard_map/all_to_all | solution.py:9
  (151 shorter events, 55.6 us)
Async XLA Ops:
  6.5 357.4 %copy-start = (bf16[4096,128]{1,0:T(8,128)(2,1)S(1)}, bf16[4096,128]{1,0:T(8,128)(2,1)}, u32[]{:S(2)}) copy-start(bf16[4096,128]{1,0:T(8,128)(2,1)} %param.13) | copy-start | bytes 3145732
  6.5 79.6 %all-gather.4.cloned.1.call-start = ((), (), s32[]{:S(2)}) async-start(), calls=%async_computation.1 | async-start | bytes 2162688 | tf_op jit(solution)/shard_map/all_gather | solution.py:34
  7.3 126.8 %all-gather.6.cloned.1.call-start = ((), (), s32[]{:S(2)}) async-start(), calls=%async_computation.2 | async-start | bytes 1114112 | tf_op jit(solution)/shard_map/all_gather | solution.py:43
  86.1 4.7 %copy-start.1 = (bf16[8,4096]{1,0:T(8,128)(2,1)S(1)}, bf16[8,4096]{1,0:T(8,128)(2,1)}, u32[]{:S(2)}) copy-start(bf16[8,4096]{1,0:T(8,128)(2,1)} %param.11) | copy-start | bytes 196612
  134.0 179.1 %copy-start.2 = (f32[128]{0:T(128)S(1)}, f32[128]{0:T(128)}, u32[]{:S(2)}) copy-start(f32[128]{0:T(128)} %param.12) | copy-start | bytes 1540
Sparse Core Ops, SparseCore 0:
  10.4 75.6 all-gather.3
  90.9 43.0 all-gather.5
